TPU v7x, 128 devices: a whole 4x4x4 slice. The times are simulated.
128 devices in a mesh: fsdp: 8 (over z, x_hi), tp: 16 (over x_lo, y, core).
Axes of the slice: x: 4 (x_hi: 2, x_lo: 2; x = x_hi * 2 + x_lo), y: 4, z: 4, core: 2. Of those that a mesh axis runs over, the one named last changes fastest.
Arguments:
- momentum: float32 [3584, 18432], P('fsdp', 'tp'), may hold values from -1500 to 1500
Outputs:
- update: float32 [3584, 18432], P('fsdp', 'tp')
All inputs are finite; a program needn't handle non-finite values.
Results may differ from a plain program's by a relative error of at most 0.008.
Values may be sent and summed in bfloat16 or wider, within the bound.
No kernel may reach another device: no remote copies, remote signals or barrier semaphores. Data moves between devices by JAX's collectives and lax.ppermute only.
A program may use at most 64 MiB of HBM per device.

v0:
```python
import math

import jax
import jax.numpy as jnp
from jax import lax
from jax.sharding import PartitionSpec as P

ROUNDS = 2


coef_linear = 3.4445
coef_cubic = -4.775
coef_quintic = 2.0315


def body(momentum):
    col_count = momentum.shape[1]
    local_squares = jnp.sum(momentum * momentum)
    squares = lax.psum(local_squares, ("fsdp", "tp"))
    scaled = (momentum / (jnp.sqrt(squares) + 1e-07)).astype(jnp.bfloat16)
    updated = scaled.astype(jnp.float32)
    for turn_index in range(ROUNDS):
        column_panel = lax.all_gather(scaled, "fsdp", axis=0, tiled=True)
        partial_value = lax.dot_general(
            scaled, column_panel, (((1,), (1,)), ((), ())), preferred_element_type=jnp.float32
        )
        share = lax.psum_scatter(
            partial_value.astype(jnp.bfloat16), "tp", scatter_dimension=1, tiled=True
        )
        row_panel = lax.all_gather(share, "tp", axis=1, tiled=True)
        square = jnp.dot(
            row_panel,
            lax.all_gather(share, "fsdp", axis=0, tiled=True),
            preferred_element_type=jnp.float32,
        )
        step_block = (coef_cubic * share.astype(jnp.float32) + coef_quintic * square).astype(
            jnp.bfloat16
        )
        product = jnp.dot(
            lax.all_gather(step_block, "tp", axis=1, tiled=True),
            column_panel,
            preferred_element_type=jnp.float32,
        )
        updated = coef_linear * scaled.astype(jnp.float32) + product
        if turn_index + 1 < ROUNDS:
            scaled = updated.astype(jnp.bfloat16)
    return updated * math.sqrt(col_count * lax.axis_size("tp"))


def solution(mesh):
    placed = (P("fsdp", "tp"),)
    return jax.shard_map(
        body, mesh=mesh, in_specs=placed, out_specs=P("fsdp", "tp"), check_vma=False
    )
```

profile of v0, /device:TPU:1, one launch (start us, length us, event | category | flops | bytes accessed | tf_op | source)
XLA Modules:
  0.0 730.1 jit_solution(10297774388623832068)
XLA Ops:
  6.5 2.7 multiply_reduce_fusion
  9.3 68.7 %psum.7 = f32[]{:T(128)} all-reduce(f32[]{:T(128)} %multiply_reduce_fusion), channel_id=1, replica_groups=mesh['fsdp'=8,'tp'=16] {'fsdp','tp'}, use_global_device_ids=true, to_apply=%region_1.0 | all-reduce | flops 1 | bytes 8 | tf_op jit(solution)/shard_map/psum | solution.py:19
  78.6 2.7 divide_convert_fusion
  81.4 102.2 %all-gather.9.cloned.1.call-done = bf16[3584,1152]{1,0:T(8,128)(2,1)} async-done(((bf16[448,1152]{1,0:T(8,128)(2,1)}), bf16[3584,1152]{1,0:T(8,128)(2,1)}) %all-gather.9.cloned.1.call-update) | async-done | bytes 8257552 | tf_op jit(solution)/shard_map/all_gather | solution.py:23
  183.6 8.0 %convolution_convert_fusion.1 = bf16[448,3584]{1,0:T(8,128)(2,1)S(1)} fusion(bf16[448,1152]{1,0:T(8,128)(2,1)} %divide_convert_fusion, bf16[3584,1152]{1,0:T(8,128)(2,1)} %all-gather.9.cloned.1.call-done), kind=kOutput, calls=%fused_computation.1 | convolution fusion | flops 3700981760 | bytes 12500992 | tf_op jit(solution)/shard_map/dot_general | solution.py:24
  191.6 3.7 copy.6
  195.4 60.4 %reduce-scatter.7.cloned.1.call-done = bf16[224,448]{1,0:T(8,128)(2,1)} async-done(((bf16[3584,448]{1,0:T(8,128)(2,1)}), bf16[224,448]{1,0:T(8,128)(2,1)}) %reduce-scatter.7.cloned.1.call-update) | async-done | bytes 200720
  255.7 1.8 copy.7
  258.2 53.7 %all-gather.13.cloned.1.call-done = bf16[3584,224]{1,0:T(8,128)(2,1)} async-done(((bf16[448,224]{1,0:T(8,128)(2,1)}), bf16[3584,224]{1,0:T(8,128)(2,1)}) %all-gather.13.cloned.1.call-update) | async-done | bytes 1605648 | tf_op jit(solution)/shard_map/all_gather | solution.py:33
  311.8 37.2 %all-gather.11.cloned.1.call-done = bf16[448,3584]{0,1:T(8,128)(2,1)} async-done(((bf16[448,224]{0,1:T(8,128)(2,1)}), bf16[448,3584]{0,1:T(8,128)(2,1)}) %all-gather.11.cloned.1.call-update) | async-done | bytes 3211280 | tf_op jit(solution)/shard_map/all_gather | solution.py:30
  349.0 3.9 fusion.5
  352.9 0.8 copy.3
  353.8 36.9 %all-gather.15.cloned.1.call-done = bf16[448,3584]{0,1:T(8,128)(2,1)} async-done(((bf16[448,224]{0,1:T(8,128)(2,1)}), bf16[448,3584]{0,1:T(8,128)(2,1)}) %all-gather.15.cloned.1.call-update) | async-done | bytes 3211280 | tf_op jit(solution)/shard_map/all_gather | solution.py:40
  390.7 9.8 %fusion.1 = bf16[448,1152]{1,0:T(8,128)(2,1)} fusion(bf16[448,3584]{0,1:T(8,128)(2,1)} %all-gather.15.cloned.1.call-done, bf16[3584,1152]{1,0:T(8,128)(2,1)} %all-gather.9.cloned.1.call-done, bf16[448,1152]{1,0:T(8,128)(2,1)S(1)} %copy-done), kind=kOutput, calls=%fused_computation.5 | convolution fusion | flops 3701440512 | bytes 13533184 | tf_op jit(solution)/shard_map/dot_general | solution.py:39
  400.7 105.3 %all-gather.17.cloned.1.call-done = bf16[3584,1152]{1,0:T(8,128)(2,1)} async-done(((bf16[448,1152]{1,0:T(8,128)(2,1)}), bf16[3584,1152]{1,0:T(8,128)(2,1)}) %all-gather.17.cloned.1.call-update) | async-done | bytes 8257552 | tf_op jit(solution)/shard_map/all_gather | solution.py:23
  506.0 8.0 %convolution_convert_fusion = bf16[448,3584]{1,0:T(8,128)(2,1)S(1)} fusion(bf16[448,1152]{1,0:T(8,128)(2,1)} %fusion.1, bf16[3584,1152]{1,0:T(8,128)(2,1)} %all-gather.17.cloned.1.call-done), kind=kOutput, calls=%fused_computation | convolution fusion | flops 3700981760 | bytes 12500992 | tf_op jit(solution)/shard_map/dot_general | solution.py:24
  514.0 3.7 copy.8
  517.8 60.4 %reduce-scatter.9.cloned.1.call-done = bf16[224,448]{1,0:T(8,128)(2,1)} async-done(((bf16[3584,448]{1,0:T(8,128)(2,1)}), bf16[224,448]{1,0:T(8,128)(2,1)}) %reduce-scatter.9.cloned.1.call-update) | async-done | bytes 200720
  578.2 1.8 copy.9
  580.7 53.4 %all-gather.21.cloned.1.call-done = bf16[3584,224]{1,0:T(8,128)(2,1)} async-done(((bf16[448,224]{1,0:T(8,128)(2,1)}), bf16[3584,224]{1,0:T(8,128)(2,1)}) %all-gather.21.cloned.1.call-update) | async-done | bytes 1605648 | tf_op jit(solution)/shard_map/all_gather | solution.py:33
  634.1 37.3 %all-gather.19.cloned.1.call-done = bf16[448,3584]{0,1:T(8,128)(2,1)} async-done(((bf16[448,224]{0,1:T(8,128)(2,1)}), bf16[448,3584]{0,1:T(8,128)(2,1)}) %all-gather.19.cloned.1.call-update) | async-done | bytes 3211280 | tf_op jit(solution)/shard_map/all_gather | solution.py:30
  671.5 3.9 fusion.4
  676.2 36.9 %all-gather.23.cloned.1.call-done = bf16[448,3584]{0,1:T(8,128)(2,1)} async-done(((bf16[448,224]{0,1:T(8,128)(2,1)}), bf16[448,3584]{0,1:T(8,128)(2,1)}) %all-gather.23.cloned.1.call-update) | async-done | bytes 3211280 | tf_op jit(solution)/shard_map/all_gather | solution.py:40
  713.2 10.1 %fusion = f32[448,1152]{1,0:T(8,128)} fusion(bf16[448,3584]{0,1:T(8,128)(2,1)} %all-gather.23.cloned.1.call-done, bf16[3584,1152]{1,0:T(8,128)(2,1)} %all-gather.17.cloned.1.call-done, bf16[448,1152]{1,0:T(8,128)(2,1)S(1)} %copy-done.1), kind=kOutput, calls=%fused_computation.3 | convolution fusion | flops 3701440512 | bytes 14565376 | tf_op jit(solution)/shard_map/dot_general | solution.py:39
  (25 shorter events, 2.7 us)
Async XLA Ops:
  6.5 177.0 %all-gather.9.cloned.1.call-start = ((), (), s32[]{:S(2)}) async-start(), calls=%async_computation.2 | async-start | bytes 9289728 | tf_op jit(solution)/shard_map/all_gather | solution.py:23
  81.3 174.4 %reduce-scatter.7.cloned.1.call-start = ((), (), s32[]{:S(2)}) async-start(), calls=%async_computation.10 | async-start | bytes 3899392
  195.3 116.5 %all-gather.13.cloned.1.call-start = ((), (), s32[]{:S(2)}) async-start(), calls=%async_computation.4 | async-start | bytes 2064384 | tf_op jit(solution)/shard_map/all_gather | solution.py:33
  257.5 91.5 %all-gather.11.cloned.1.call-start = ((), (), s32[]{:S(2)}) async-start(), calls=%async_computation.3 | async-start | bytes 3899392 | tf_op jit(solution)/shard_map/all_gather | solution.py:30
  258.1 132.6 %copy-start = (bf16[448,1152]{1,0:T(8,128)(2,1)S(1)}, bf16[448,1152]{1,0:T(8,128)(2,1)}, u32[]{:S(2)}) copy-start(bf16[448,1152]{1,0:T(8,128)(2,1)} %divide_convert_fusion) | copy-start | bytes 3096580
  258.1 132.6 %all-gather.15.cloned.1.call-start = ((), (), s32[]{:S(2)}) async-start(), calls=%async_computation.5 | async-start | bytes 3899392 | tf_op jit(solution)/shard_map/all_gather | solution.py:40
  353.8 152.2 %all-gather.17.cloned.1.call-start = ((), (), s32[]{:S(2)}) async-start(), calls=%async_computation.6 | async-start | bytes 9289728 | tf_op jit(solution)/shard_map/all_gather | solution.py:23
  400.5 177.7 %reduce-scatter.9.cloned.1.call-start = ((), (), s32[]{:S(2)}) async-start(), calls=%async_computation.11 | async-start | bytes 3899392
  517.7 116.4 %all-gather.21.cloned.1.call-start = ((), (), s32[]{:S(2)}) async-start(), calls=%async_computation.8 | async-start | bytes 2064384 | tf_op jit(solution)/shard_map/all_gather | solution.py:33
  579.9 91.5 %all-gather.19.cloned.1.call-start = ((), (), s32[]{:S(2)}) async-start(), calls=%async_computation.7 | async-start | bytes 3899392 | tf_op jit(solution)/shard_map/all_gather | solution.py:30
  580.7 132.5 %copy-start.1 = (bf16[448,1152]{1,0:T(8,128)(2,1)S(1)}, bf16[448,1152]{1,0:T(8,128)(2,1)}, u32[]{:S(2)}) copy-start(bf16[448,1152]{1,0:T(8,128)(2,1)} %fusion.1) | copy-start | bytes 3096580
  580.7 132.5 %all-gather.23.cloned.1.call-start = ((), (), s32[]{:S(2)}) async-start(), calls=%async_computation.9 | async-start | bytes 3899392 | tf_op jit(solution)/shard_map/all_gather | solution.py:40
Sparse Core Ops, SparseCore 0:
  81.4 102.0 all-gather.8
  195.4 60.2 reduce-scatter.6
  258.0 53.7 all-gather.12
  313.4 35.5 all-gather.10
  353.9 36.7 all-gather.14
  400.6 105.3 all-gather.16
  517.9 60.2 reduce-scatter.8
  580.5 53.6 all-gather.20
  635.8 35.5 all-gather.18
  676.4 36.7 all-gather.22
where the time goes:
time: 730 us
  waiting for transfers between devices  585 us (80%)
  blocking collectives  68.7 us (9%)
  matrix products  43.8 us (6%)
  between operations  14.3 us (2%)
  local copies, waits for them, and re-layouts  12.6 us (2%)
    all_gather x2, waiting for transfers between devices, body(): column_panel = lax.all_gather(scaled, 'fsdp', axis=0, tiled=True)  207 us
    unnamed x12, waiting for transfers between devices  122 us
    all_gather x2, waiting for transfers between devices, body(): lax.all_gather(share, 'fsdp', axis=0, tiled=True)  107 us
    all_gather x2, waiting for transfers between devices, body(): row_panel = lax.all_gather(share, 'tp', axis=1, tiled=True)  74.5 us
    all_gather x2, waiting for transfers between devices, body(): lax.all_gather(step_block, 'tp', axis=1, tiled=True)  73.8 us
    psum x1, blocking collectives, body(): squares = lax.psum(local_squares, ('fsdp', 'tp'))  68.7 us
    dot_general x2, matrix products, body(): jnp.dot(lax.all_gather(step_block, 'tp', axis=1, tiled=True), column_pane...  19.9 us
    dot_general x2, matrix products, body(): lax.dot_general(scaled, column_panel, (((1,), (1,)), ((), ())), preferred...  16 us
  transfers between devices with their start and end apart: 10, of which 10 were waited for; matrix products, arithmetic and copies ran while one was open for 0% of the time, Pallas kernels for 0%

commit v1 on v0

v1 whole, which is shorter than its diff:
```python
import functools
import math

import jax
import jax.numpy as jnp
import numpy as np
from jax import lax
from jax.experimental import pallas as pl
from jax.experimental.pallas import tpu as pltpu
from jax.sharding import Mesh, PartitionSpec as P

coef_linear = 3.4445
coef_cubic = -4.775
coef_quintic = 2.0315

NAMES = ("z", "xh", "xl", "y", "c")
SIZES = (4, 2, 2, 4, 2)
PLANE = ("xh", "xl", "y")
BF = jnp.bfloat16
F32 = jnp.float32
ROWS = 448
SUB = 224
TAIL = 240
COLS = 1152
ALL = 3584
TILE = 128
WIDE = 512
VMEM = 60 * 1024 * 1024

def flat(pos):
    index = 0
    for value, size in zip(pos, SIZES):
        index = index * size + value
    return index


def move(value, target):
    every = [(z, a, b, y, c) for z in range(4) for a in range(2) for b in range(2) for y in range(4) for c in range(2)]
    return lax.ppermute(value, NAMES, [(flat(pos), flat(target(*pos))) for pos in every])


def swap_z(value, by):
    return move(value, lambda z, xh, xl, y, c: (z ^ by, xh, xl, y, c))


def other_core(value):
    return move(value, lambda z, xh, xl, y, c: (z, xh, xl, y, 1 - c))


def trade_roles(value):
    return move(value, lambda z, xh, xl, y, c: (z, c, xl, y, xh))


def struct(*shape, dtype=BF):
    return jax.ShapeDtypeStruct(shape, dtype)


def call(kernel, shapes, counts, name, flops, scratch=(), scalars_out=0):
    smem, vmem = counts
    n = len(shapes)
    return pl.pallas_call(
        kernel,
        out_shape=shapes,
        in_specs=[pl.BlockSpec(memory_space=pltpu.SMEM)] * smem + [pl.BlockSpec(memory_space=pltpu.VMEM)] * vmem,
        out_specs=[pl.BlockSpec(memory_space=pltpu.VMEM)] * (n - scalars_out)
        + [pl.BlockSpec(memory_space=pltpu.SMEM)] * scalars_out,
        scratch_shapes=list(scratch),
        compiler_params=pltpu.CompilerParams(vmem_limit_bytes=VMEM),
        cost_estimate=pl.CostEstimate(flops=flops, bytes_accessed=6 << 20, transcendentals=0),
        name=name,
    )


def split_value(value):
    lane = lax.broadcasted_iota(jnp.int32, (16, TILE), 1)
    whole = jnp.full((16, TILE), value, F32)
    high = whole.astype(BF).astype(F32)
    middle = (whole - high).astype(BF).astype(F32)
    low = whole - high - middle
    out = jnp.where(lane == 0, high, jnp.where(lane == 1, middle, jnp.where(lane == 2, low, 0.0)))
    return out.astype(BF)


def cast_kernel(in_ref, upper_ref, lower_ref):
    squares = jnp.zeros((8, COLS), F32)
    for i in range(0, ROWS, 32):
        block = in_ref[i : i + 32, :]
        if i < SUB:
            upper_ref[i : i + 32, :] = block.astype(BF)
        else:
            lower_ref[i - SUB : i - SUB + 32, :] = block.astype(BF)
        square = block * block
        squares += (square[:8] + square[8:16]) + (square[16:24] + square[24:])
    lower_ref[SUB:, :] = jnp.zeros((TAIL - SUB, COLS), BF)
    lower_ref[SUB:, :TILE] = split_value(jnp.sum(squares))


def cast(momentum):
    return call(cast_kernel, [struct(SUB, COLS), struct(TAIL, COLS)], (0, 1), "cast", 0)(momentum)


def pieces(refs):
    for ref in refs:
        step = ref.shape[0] // 2
        for i in range(2):
            yield ref[i * step : i * step + SUB, :]


def sum_of_squares(refs):
    total = jnp.zeros((), F32)
    for ref in refs:
        if ref.shape[0] == 2 * TAIL:
            for i in range(2):
                total += jnp.sum(ref[i * TAIL + SUB : (i + 1) * TAIL, :TILE].astype(F32)) * 0.0625
    return total


def turn(upper_ref, lower_ref, turned):
    turned[:, :SUB] = upper_ref[:SUB, :].T
    turned[:, SUB:] = lower_ref[:SUB, :].T


def gram_kernel(*refs):
    parts, out_ref, turned = refs[:-2], refs[-2], refs[-1]
    turn(parts[0], parts[1], turned)
    for i, piece in enumerate(pieces(parts)):
        out_ref[i] = jnp.dot(piece, turned[...], preferred_element_type=F32).astype(BF)


def gram(parts):
    flops = 2 * 2 * len(parts) * SUB * ROWS * COLS
    scratch = [pltpu.VMEM((COLS, ROWS), BF)]
    return call(gram_kernel, [struct(2 * len(parts), SUB, ROWS)], (0, len(parts)), "gram", flops, scratch)(*parts)[0]


def gram_more_kernel(count, order_ref, done_ref, *refs):
    parts, fresh, (out_ref, value_ref, turned) = refs[:count], refs[count : 2 * count], refs[2 * count :]
    turn(parts[0], parts[1], turned)
    for n in range(2 * count):
        out_ref[order_ref[n]] = done_ref[n]
    for n, piece in enumerate(pieces(fresh)):
        out_ref[order_ref[2 * count + n]] = jnp.dot(piece, turned[...], preferred_element_type=F32).astype(BF)
    value_ref[0] = sum_of_squares(parts) + sum_of_squares(fresh)


def gram_more(order, done, parts, fresh):
    count = len(parts)
    return call(
        functools.partial(gram_more_kernel, count),
        [struct(16, SUB, ROWS), struct(1, dtype=F32)],
        (1, 1 + 2 * count),
        "gram",
        2 * 2 * count * SUB * ROWS * COLS,
        [pltpu.VMEM((COLS, ROWS), BF)],
        scalars_out=1,
    )(order, done, *parts, *fresh)


def panel_kernel(order_ref, *refs):
    parts, out_ref = refs[:-1], refs[-1]
    for i, piece in enumerate(pieces(parts)):
        out_ref[order_ref[i]] = piece


def sum_kernel(value_ref, shares_ref, out_ref):
    total = shares_ref[0].astype(F32)
    for i in range(1, 16):
        total += shares_ref[i].astype(F32)
    out_ref[:, :ROWS] = total.astype(BF)
    out_ref[:, ROWS:] = jnp.zeros((SUB, WIDE - ROWS), BF)
    out_ref[:16, ROWS:] = split_value(value_ref[0])[:, : WIDE - ROWS]


def sum_shares(value, shares):
    return call(sum_kernel, [struct(SUB, WIDE)], (1, 1), "sum", 0)(value, shares)[0]


def fill_left(core_ref, mine_ref, other_ref, left):
    first = core_ref[0] == 0
    for i in range(4):
        mine, other = mine_ref[i, :, :ROWS], other_ref[i, :, :ROWS]
        left[:, i * 896 : i * 896 + ROWS] = jnp.where(first, mine, other)
        left[:, i * 896 + ROWS : (i + 1) * 896] = jnp.where(first, other, mine)


def first_kernel(core_ref, mine_ref, other_ref, right_ref, share_ref, out_ref, weight_ref, left):
    squares = jnp.zeros((), F32)
    for i in range(16):
        squares += jnp.sum(right_ref[i * SUB : i * SUB + 16, ROWS:].astype(F32)) * 0.0625
    scale = 1.0 / (jnp.sqrt(jnp.full((8, TILE), squares, F32)) + 1e-07)
    scale = jnp.max(scale)
    twice = scale * scale
    fill_left(core_ref, mine_ref, other_ref, left)
    total = jnp.dot(left[...], right_ref[:, :ROWS], preferred_element_type=F32)
    total = total * twice * (coef_quintic * twice) + (coef_cubic * twice) * share_ref[:, :ROWS].astype(F32)
    out_ref[...] = total.astype(BF)
    weight_ref[0] = twice
    weight_ref[1] = coef_linear * twice
    weight_ref[2] = scale * math.sqrt(18432)


def first_mul(core, lefts, right, share):
    return call(
        first_kernel,
        [struct(SUB, ROWS), struct(3, dtype=F32)],
        (1, 4),
        "first_mul",
        2 * SUB * ROWS * ALL,
        [pltpu.VMEM((SUB, ALL), BF)],
        scalars_out=1,
    )(core, *lefts, right, share)


def mul_kernel(weights, core_ref, weight_ref, mine_ref, other_ref, right_ref, *refs):
    extras, out_ref, left = refs[:-2], refs[-2], refs[-1]
    if weights is None:
        weights = [weight_ref[0], weight_ref[1]]
    fill_left(core_ref, mine_ref, other_ref, left)
    total = jnp.dot(left[...], right_ref[:, :ROWS], preferred_element_type=F32) * weights[0]
    for weight, extra in zip(weights[1:], extras):
        total += weight * extra[:, :ROWS].astype(F32)
    out_ref[...] = total.astype(BF)


def mul(core, weight, lefts, right, weights, extras):
    return call(
        functools.partial(mul_kernel, weights),
        [struct(SUB, ROWS)],
        (2, 3 + len(extras)),
        "mul",
        2 * SUB * ROWS * ALL,
        [pltpu.VMEM((SUB, ALL), BF)],
    )(core, weight, *lefts, right, *extras)[0]


def apply_kernel(weight_ref, upper_ref, lower_ref, panel_ref, right_ref, out_ref, send_ref, mat):
    for k in range(8):
        mat[:, k * ROWS : (k + 1) * ROWS] = right_ref[k * ROWS : (k + 1) * ROWS, :].T
    linear = coef_linear * coef_linear
    for i, own in ((0, upper_ref), (SUB, lower_ref)):
        total = jnp.dot(mat[i : i + SUB, :], panel_ref[...], preferred_element_type=F32)
        total = (total + linear * own[:SUB, :].astype(F32)) * weight_ref[2]
        out_ref[i : i + SUB, :] = total
        send_ref[i : i + SUB, :] = total.astype(BF)


def apply(weight, upper, lower, panel, right):
    return call(
        apply_kernel,
        [struct(ROWS, COLS, dtype=F32), struct(ROWS, COLS)],
        (1, 4),
        "apply",
        2 * ALL * ROWS * COLS,
        [pltpu.VMEM((ROWS, ALL), BF)],
    )(weight, upper, lower, panel, right)


def gather_rows(value):
    mine = lax.all_gather(value, "z")
    return [mine, other_core(mine)]


def gather_plane(value):
    return lax.all_gather(value, PLANE, axis=0, tiled=True)


def body(momentum):
    z, c = (lax.axis_index(name).astype(jnp.int32) for name in ("z", "c"))
    same = lax.axis_index("xh") == c
    core = c.reshape(1)

    upper, lower = (trade_roles(value) for value in cast(momentum))
    upper_1 = swap_z(upper, 1)
    lower_3 = swap_z(lower, 3)
    uppers = jnp.concatenate([upper, upper_1], 0)
    lowers = jnp.concatenate([lower, lower_3], 0)
    uppers_3 = swap_z(uppers, 3)
    lowers_1 = swap_z(lowers, 1)
    early = [uppers, lowers, other_core(uppers), other_core(lowers)]
    done = gram(early)
    uppers_3, lowers_1, done = lax.optimization_barrier((uppers_3, lowers_1, done))
    late = [uppers_3, lowers_1, other_core(uppers_3), other_core(lowers_1)]
    early_at = [(by, swap, half) for swap in (0, 1) for half in (0, 1) for by in ((0, 1) if half == 0 else (0, 3))]
    late_at = [(by, swap, half) for swap in (0, 1) for half in (0, 1) for by in ((3, 2) if half == 0 else (1, 2))]
    by, swap, half = (np.array(column, np.int32) for column in zip(*(early_at + late_at)))
    piece_x = z ^ by
    piece_y = (c ^ swap) * 2 + half
    order = piece_x * 4 + piece_y

    partial, value = gram_more(order, done, early, late)
    a = sum_shares(value, lax.all_to_all(partial, PLANE, 0, 0, tiled=True))
    panel = call(panel_kernel, [struct(16, SUB, COLS)], (1, 8), "panel", 0)(order, *early, *late)[0]
    panel = panel.reshape(ALL, COLS)

    a_right = gather_plane(a)
    b, weight = first_mul(core, gather_rows(a), a_right, a)

    b_right = gather_plane(b)
    v = mul(core, weight, gather_rows(b), a_right, None, (a,))
    a2 = mul(core, weight, gather_rows(v), b_right, (1.0, coef_linear), (v,))

    a2_right = gather_plane(a2)
    h = mul(core, weight, gather_rows(a2), b_right, (1.0, coef_linear), (a2,))
    d = mul(core, weight, gather_rows(h), a2_right, (coef_quintic, coef_cubic, coef_linear), (h, b))

    update, sent = apply(weight, upper, lower, panel, gather_plane(d))
    return jnp.where(same, update, trade_roles(sent).astype(F32))


def solution(mesh):
    split = Mesh(mesh.devices.reshape(SIZES), NAMES)
    placed = P(("z", "xh"), ("xl", "y", "c"))
    return jax.shard_map(body, mesh=split, in_specs=(placed,), out_specs=placed, check_vma=False)
```

time: 730 us -> 382 us (0.52)
  waiting for transfers between devices: 585 us -> 142 us
  Pallas kernels: 0 us -> 62.4 us
  blocking collectives: 68.7 us -> 118 us
  matrix products: 43.8 us -> 0 us
  starting transfers between devices: 0.55 us -> 37.2 us
    all_gather x8 -> x4, waiting for transfers between devices: 463 us -> 87.6 us  [gather_plane(): return lax.all_gather(value, PLANE, axis=0, tiled=True)]
    unnamed x12 -> x4, waiting for transfers between devices: 122 us -> 0.07 us
    psum x1 -> x0, blocking collectives: 68.7 us -> none  [body(): squares = lax.psum(local_squares, ('fsdp', 'tp'))]
    all_gather x0 -> x5, blocking collectives: none -> 65.6 us  [gather_rows(): mine = lax.all_gather(value, 'z')]
    pallas_call x0 -> x11, Pallas kernels: none -> 62.4 us  [the longest x4 17.3 us: mul(): call(functools.partial(mul_kernel, weights), [struct(SUB, ROWS)], (2, 3 +...]
    ppermute x0 -> x16, waiting for transfers between devices: none -> 54.4 us  [move(): lax.ppermute(value, NAMES, [(flat(pos), flat(target(*pos))) for pos in ev...]
    all_to_all x0 -> x1, blocking collectives: none -> 52.6 us  [body(): a = sum_shares(value, lax.all_to_all(partial, PLANE, 0, 0, tiled=True))]
    dot_general x6 -> x0, matrix products: 43.8 us -> none  [the longest x2 19.9 us: body(): jnp.dot(lax.all_gather(step_block, 'tp', axis=1, tiled=True), column_pane...]
  transfers between devices with their start and end apart: 10 -> 20, of which waited for: 10 -> 16; matrix products, arithmetic and copies ran while one was open for 0% -> 0% of each run, Pallas kernels for 0% -> 6%
where the time goes in v1:
time: 382 us; the launch traced here: 381 us
  waiting for transfers between devices  142 us (37%)
  blocking collectives  118 us (31%)
  Pallas kernels  62.4 us (16%)
  starting transfers between devices  37.2 us (10%)
  between operations  13.3 us (3%)
  local copies, waits for them, and re-layouts  6.16 us (2%)
    all_gather x4, waiting for transfers between devices, gather_plane(): return lax.all_gather(value, PLANE, axis=0, tiled=True)  87.6 us
    all_gather x5, blocking collectives, gather_rows(): mine = lax.all_gather(value, 'z')  65.6 us
    ppermute x16, waiting for transfers between devices, move(): lax.ppermute(value, NAMES, [(flat(pos), flat(target(*pos))) for pos in ev...  54.4 us
    all_to_all x1, blocking collectives, body(): a = sum_shares(value, lax.all_to_all(partial, PLANE, 0, 0, tiled=True))  52.6 us
    ppermute x16, starting transfers between devices, move(): lax.ppermute(value, NAMES, [(flat(pos), flat(target(*pos))) for pos in ev...  37.1 us
    pallas_call x4, Pallas kernels, mul(): call(functools.partial(mul_kernel, weights), [struct(SUB, ROWS)], (2, 3 +...  17.3 us
    pallas_call x1, Pallas kernels, apply(): call(apply_kernel, [struct(ROWS, COLS, dtype=F32), struct(ROWS, COLS)], (...  11.3 us
    pallas_call x1, Pallas kernels, gram_more(): call(functools.partial(gram_more_kernel, count), [struct(16, SUB, ROWS),...  8.78 us
  transfers between devices with their start and end apart: 20, of which 16 were waited for; matrix products, arithmetic and copies ran while one was open for 0% of the time, Pallas kernels for 6%

profile of v1, /device:TPU:1, one launch (start us, length us, event | category | flops | bytes accessed | tf_op | source)
XLA Modules:
  0.0 381.4 jit_solution(14597037428933507031)
XLA Ops:
  9.2 6.0 %collective-permute-start.3 = (bf16[240,1152]{1,0:T(8,128)(2,1)}, bf16[240,1152]{1,0:T(8,128)(2,1)S(1)}, u32[]{:S(2)}, u32[]{:S(2)}) collective-permute-start(bf16[240,1152]{1,0:T(8,128)(2,1)} %get-tuple-element.17), channel_id=1, source_target_pairs={{0,0},{1,16},{2,2},{3,18},{4,4},{5,20},{6,6},{7,22},{8,8},{9,24},{... | collective-permute-start | bytes 1658888 | tf_op jit(solution)/shard_map/ppermute | solution.py:39
  17.2 5.4 %collective-permute-done.3.lower_ref = bf16[240,1152]{1,0:T(8,128)(2,1)S(1)} collective-permute-done((bf16[240,1152]{1,0:T(8,128)(2,1)}, bf16[240,1152]{1,0:T(8,128)(2,1)S(1)}, u32[]{:S(2)}, u32[]{:S(2)}) %collective-permute-start.3) | collective-permute-done | bytes 552992 | tf_op jit(solution)/shard_map/ppermute | solution.py:39
  42.3 6.4 %gram.2.done_ref = bf16[8,224,448]{2,1,0:T(8,128)(2,1)} custom-call(bf16[448,1152]{1,0:T(8,128)(2,1)} %copy-done.1, bf16[480,1152]{1,0:T(8,128)(2,1)} %copy-done, bf16[448,1152]{1,0:T(8,128)(2,1)} %copy-done.4, bf16[480,1152]{1,0:T(8,128)(2,1)} %copy-done.2), custom_call_target="tpu_custom_call" | custom-call | flops 1849688064 | bytes 6291456 | tf_op jit(solution)/shard_map/gram/pallas_call | solution.py:133
  48.6 14.4 %collective-permute-done.2.refs_4_ = bf16[448,1152]{1,0:T(8,128)(2,1)} collective-permute-done((bf16[448,1152]{1,0:T(8,128)(2,1)S(1)}, bf16[448,1152]{1,0:T(8,128)(2,1)}, u32[]{:S(2)}, u32[]{:S(2)}) %collective-permute-start.2) | collective-permute-done | bytes 1032224 | tf_op jit(solution)/shard_map/ppermute | solution.py:39
  70.6 8.8 %gram.3 = (bf16[16,224,448]{2,1,0:T(8,128)(2,1)}, f32[1]{0:T(128)}) custom-call(s32[16]{0:T(128)} %add_add_fusion.order_ref, bf16[8,224,448]{2,1,0:T(8,128)(2,1)} %gram.2.done_ref, bf16[448,1152]{1,0:T(8,128)(2,1)} %copy-done.1, bf16[480,1152]{1,0:T(8,128)(2,1)} %copy-done, bf16[448,1152]{1,0:T(8,128)(2,1)} %copy-done.4, bf16[480,1152]{1,0:T(8,128)(2,1)} %copy-done.2, ...), custom_call_target="tpu_custom_call" | custom-call | flops 1849688064 | bytes 6291456 | tf_op jit(solution)/shard_map/gram/pallas_call | solution.py:148
  79.4 52.6 %all_to_all.5.shares_ref = bf16[16,224,448]{2,1,0:T(8,128)(2,1)} all-to-all(bf16[16,224,448]{2,1,0:T(8,128)(2,1)} %get-tuple-element.22), channel_id=1, replica_groups=mesh['z'=4,'xh'=2,'xl'=2,'y'=4,'c'=2] {'xh','xl','y'}, dimensions={0} | all-to-all | bytes 6422528 | tf_op jit(solution)/shard_map/all_to_all | solution.py:291
  136.3 11.4 %all-gather = bf16[896,512]{1,0:T(8,128)(2,1)S(1)} all-gather(bf16[224,512]{1,0:T(8,128)(2,1)} %sum.1.share_ref.refs_0_), channel_id=2, replica_groups=mesh['z'=4,'xh'=2,'xl'=2,'y'=4,'c'=2] {'z'}, dimensions={0}, use_global_device_ids=true | all-gather | bytes 1146880 | tf_op jit(solution)/shard_map/all_gather | solution.py:259
  147.7 5.3 %collective-permute-start.10 = (bf16[4,224,512]{2,1,0:T(8,128)(2,1)S(1)}, bf16[4,224,512]{2,1,0:T(8,128)(2,1)S(1)}, u32[]{:S(2)}, u32[]{:S(2)}) collective-permute-start(bf16[4,224,512]{2,1,0:T(8,128)(2,1)S(1)} %bitcast.16), channel_id=1, source_target_pairs={{0,1},{1,0},{2,3},{3,2},{4,5},{5,4},{6,7},{7,6},{8,9},{9,8},{10,11... | collective-permute-start | bytes 2752520 | tf_op jit(solution)/shard_map/ppermute | solution.py:39
  155.1 29.4 %all-gather.10.cloned.1.call-done.right_ref = bf16[3584,512]{1,0:T(8,128)(2,1)} async-done(((bf16[224,512]{1,0:T(8,128)(2,1)}), bf16[3584,512]{1,0:T(8,128)(2,1)}) %all-gather.10.cloned.1.call-update) | async-done | bytes 3670032 | tf_op jit(solution)/shard_map/all_gather | solution.py:264
  184.5 4.4 %first_mul.1 = (bf16[224,448]{1,0:T(8,128)(2,1)}, f32[3]{0:T(128)}) custom-call(s32[1]{0:T(128)} %bitcast.core_ref, bf16[4,224,512]{2,1,0:T(8,128)(2,1)} %bitcast.17, bf16[4,224,512]{2,1,0:T(8,128)(2,1)} %copy-done.15, bf16[3584,512]{1,0:T(8,128)(2,1)} %all-gather.10.cloned.1.call-done.right_ref, bf16[224,512]{1,0:T(8,128)(2,1)} %sum.1.share_ref.refs_0_), custom_call_target="tpu_custom_call" | custom-call | flops 719323136 | bytes 6291456 | tf_op jit(solution)/shard_map/first_mul/pallas_call | solution.py:203
  188.9 13.4 %all-gather.1 = bf16[896,448]{1,0:T(8,128)(2,1)S(1)} all-gather(bf16[224,448]{1,0:T(8,128)(2,1)} %get-tuple-element.24.refs_1_), channel_id=3, replica_groups=mesh['z'=4,'xh'=2,'xl'=2,'y'=4,'c'=2] {'z'}, dimensions={0}, use_global_device_ids=true | all-gather | bytes 1003520 | tf_op jit(solution)/shard_map/all_gather | solution.py:259
  207.6 4.3 %mul.14.refs_0_ = bf16[224,448]{1,0:T(8,128)(2,1)} custom-call(s32[1]{0:T(128)} %bitcast.core_ref, f32[3]{0:T(128)} %get-tuple-element.23.weight_ref, bf16[4,224,448]{2,1,0:T(8,128)(2,1)} %bitcast.13, bf16[4,224,448]{2,1,0:T(8,128)(2,1)} %copy-done.13, bf16[3584,512]{1,0:T(8,128)(2,1)} %all-gather.10.cloned.1.call-done.right_ref, ...), custom_call_target="tpu_custom_call" | custom-call | flops 719323136 | bytes 6291456 | tf_op jit(solution)/shard_map/mul/pallas_call | solution.py:226
  211.9 13.7 %all-gather.2 = bf16[896,448]{1,0:T(8,128)(2,1)S(1)} all-gather(bf16[224,448]{1,0:T(8,128)(2,1)} %mul.14.refs_0_), channel_id=4, replica_groups=mesh['z'=4,'xh'=2,'xl'=2,'y'=4,'c'=2] {'z'}, dimensions={0}, use_global_device_ids=true | all-gather | bytes 1003520 | tf_op jit(solution)/shard_map/all_gather | solution.py:259
  229.5 8.3 %all-gather.12.cloned.1.call-done.right_ref = bf16[3584,448]{1,0:T(8,128)(2,1)} async-done(((bf16[224,448]{1,0:T(8,128)(2,1)}), bf16[3584,448]{1,0:T(8,128)(2,1)}) %all-gather.12.cloned.1.call-update) | async-done | bytes 3211280 | tf_op jit(solution)/shard_map/all_gather | solution.py:264
  242.2 13.4 %all-gather.3 = bf16[896,448]{1,0:T(8,128)(2,1)S(1)} all-gather(bf16[224,448]{1,0:T(8,128)(2,1)} %mul.15.refs_0_), channel_id=5, replica_groups=mesh['z'=4,'xh'=2,'xl'=2,'y'=4,'c'=2] {'z'}, dimensions={0}, use_global_device_ids=true | all-gather | bytes 1003520 | tf_op jit(solution)/shard_map/all_gather | solution.py:259
  260.9 4.3 %mul.16.refs_0_ = bf16[224,448]{1,0:T(8,128)(2,1)} custom-call(s32[1]{0:T(128)} %bitcast.core_ref, f32[3]{0:T(128)} %get-tuple-element.23.weight_ref, bf16[4,224,448]{2,1,0:T(8,128)(2,1)} %bitcast.15, bf16[4,224,448]{2,1,0:T(8,128)(2,1)} %copy-done.14, bf16[3584,448]{1,0:T(8,128)(2,1)} %all-gather.12.cloned.1.call-done.right_ref, bf16[224,448]{1,0:T(8,128)(2,1)} %mul.15.refs_0_), custom_call_target="tpu_custom_call" | custom-call | flops 719323136 | bytes 6291456 | tf_op jit(solution)/shard_map/mul/pallas_call | solution.py:226
  265.2 13.7 %all-gather.4 = bf16[896,448]{1,0:T(8,128)(2,1)S(1)} all-gather(bf16[224,448]{1,0:T(8,128)(2,1)} %mul.16.refs_0_), channel_id=6, replica_groups=mesh['z'=4,'xh'=2,'xl'=2,'y'=4,'c'=2] {'z'}, dimensions={0}, use_global_device_ids=true | all-gather | bytes 1003520 | tf_op jit(solution)/shard_map/all_gather | solution.py:259
  282.7 8.3 %all-gather.14.cloned.1.call-done.right_ref = bf16[3584,448]{1,0:T(8,128)(2,1)} async-done(((bf16[224,448]{1,0:T(8,128)(2,1)}), bf16[3584,448]{1,0:T(8,128)(2,1)}) %all-gather.14.cloned.1.call-update) | async-done | bytes 3211280 | tf_op jit(solution)/shard_map/all_gather | solution.py:264
  291.1 4.4 %mul.17 = bf16[224,448]{1,0:T(8,128)(2,1)} custom-call(s32[1]{0:T(128)} %bitcast.core_ref, f32[3]{0:T(128)} %get-tuple-element.23.weight_ref, bf16[4,224,448]{2,1,0:T(8,128)(2,1)} %bitcast.9, bf16[4,224,448]{2,1,0:T(8,128)(2,1)} %copy-done.11, bf16[3584,448]{1,0:T(8,128)(2,1)} %all-gather.14.cloned.1.call-done.right_ref, bf16[224,448]{1,0:T(8,128)(2,1)} %mul.16.refs_0_, ...), custom_call_target="tpu_custom_call" | custom-call | flops 719323136 | bytes 6291456 | tf_op jit(solution)/shard_map/mul/pallas_call | solution.py:226
  295.5 7.3 %panel.1 = bf16[16,224,1152]{2,1,0:T(8,128)(2,1)} custom-call(s32[16]{0:T(128)} %add_add_fusion.order_ref, bf16[448,1152]{1,0:T(8,128)(2,1)} %copy-done.1, bf16[480,1152]{1,0:T(8,128)(2,1)} %copy-done, bf16[448,1152]{1,0:T(8,128)(2,1)} %copy-done.4, bf16[480,1152]{1,0:T(8,128)(2,1)} %copy-done.2, bf16[448,1152]{1,0:T(8,128)(2,1)} %collective-permute-done.2.refs_4_, ...), custom_call_target="tpu_custom_call" | custom-call | bytes 6291456 | tf_op jit(solution)/shard_map/panel/pallas_call | solution.py:292
  302.8 41.6 %all-gather.16.cloned.1.call-done.right_ref = bf16[3584,448]{1,0:T(8,128)(2,1)} async-done(((bf16[224,448]{1,0:T(8,128)(2,1)}), bf16[3584,448]{1,0:T(8,128)(2,1)}) %all-gather.16.cloned.1.call-update) | async-done | bytes 3211280 | tf_op jit(solution)/shard_map/all_gather | solution.py:264
  344.4 11.3 %apply.1 = (f32[448,1152]{1,0:T(8,128)}, bf16[448,1152]{1,0:T(8,128)(2,1)}) custom-call(f32[3]{0:T(128)} %get-tuple-element.23.weight_ref, bf16[224,1152]{1,0:T(8,128)(2,1)} %copy-done.17, bf16[240,1152]{1,0:T(8,128)(2,1)} %copy-done.16, bf16[3584,1152]{1,0:T(8,128)(2,1)} %bitcast.7, bf16[3584,448]{1,0:T(8,128)(2,1)} %all-gather.16.cloned.1.call-done.right_ref), custom_call_target="tpu_custom_call" | custom-call | flops 3699376128 | bytes 6291456 | tf_op jit(solution)/shard_map/apply/pallas_call | solution.py:248
  355.7 5.1 %collective-permute-start.15 = (bf16[448,1152]{1,0:T(8,128)(2,1)}, bf16[448,1152]{1,0:T(8,128)(2,1)S(1)}, u32[]{:S(2)}, u32[]{:S(2)}) collective-permute-start(bf16[448,1152]{1,0:T(8,128)(2,1)} %get-tuple-element.26), channel_id=1, source_target_pairs={{0,0},{1,16},{2,2},{3,18},{4,4},{5,20},{6,6},{7,22},{8,8},{9,24},{... | collective-permute-start | bytes 3096584 | tf_op jit(solution)/shard_map/ppermute | solution.py:39
  360.8 12.6 %collective-permute-done.15 = bf16[448,1152]{1,0:T(8,128)(2,1)S(1)} collective-permute-done((bf16[448,1152]{1,0:T(8,128)(2,1)}, bf16[448,1152]{1,0:T(8,128)(2,1)S(1)}, u32[]{:S(2)}, u32[]{:S(2)}) %collective-permute-start.15) | collective-permute-done | bytes 1032224 | tf_op jit(solution)/shard_map/ppermute | solution.py:39
  (85 shorter events, 62.2 us)
Async XLA Ops:
  6.5 177.9 %all-gather.10.cloned.1.call-start = ((), (), s32[]{:S(2)}) async-start(), calls=%async_computation.1 | async-start | bytes 3899392 | tf_op jit(solution)/shard_map/all_gather | solution.py:264
  9.2 13.4 %collective-permute-start.3 = (bf16[240,1152]{1,0:T(8,128)(2,1)}, bf16[240,1152]{1,0:T(8,128)(2,1)S(1)}, u32[]{:S(2)}, u32[]{:S(2)}) collective-permute-start(bf16[240,1152]{1,0:T(8,128)(2,1)} %get-tuple-element.17), channel_id=1, source_target_pairs={{0,0},{1,16},{2,2},{3,18},{4,4},{5,20},{6,6},{7,22},{8,8},{9,24},{... | collective-permute-start | bytes 1658888 | tf_op jit(solution)/shard_map/ppermute | solution.py:39
  15.3 12.9 %collective-permute-start = (bf16[224,1152]{1,0:T(8,128)(2,1)}, bf16[224,1152]{1,0:T(8,128)(2,1)S(1)}, u32[]{:S(2)}, u32[]{:S(2)}) collective-permute-start(bf16[224,1152]{1,0:T(8,128)(2,1)} %get-tuple-element.16), channel_id=1, source_target_pairs={{0,0},{1,16},{2,2},{3,18},{4,4},{5,20},{6,6},{7,22},{8,8},{9,24},{... | collective-permute-start | bytes 1548296 | tf_op jit(solution)/shard_map/ppermute | solution.py:39
  22.6 10.6 %collective-permute-start.4 = (bf16[240,1152]{1,0:T(8,128)(2,1)S(1)}, bf16[240,1152]{1,0:T(8,128)(2,1)S(1)}, u32[]{:S(2)}, u32[]{:S(2)}) collective-permute-start(bf16[240,1152]{1,0:T(8,128)(2,1)S(1)} %collective-permute-done.3.lower_ref), channel_id=1, source_target_pairs={{0,96},{1,97},{2,98},{3,99},{4,100},{5,101},{6,102},{7,103},{8,104... | collective-permute-start | bytes 1658888 | tf_op jit(solution)/shard_map/ppermute | solution.py:39
  28.2 8.1 %collective-permute-start.1 = (bf16[224,1152]{1,0:T(8,128)(2,1)S(1)}, bf16[224,1152]{1,0:T(8,128)(2,1)S(1)}, u32[]{:S(2)}, u32[]{:S(2)}) collective-permute-start(bf16[224,1152]{1,0:T(8,128)(2,1)S(1)} %collective-permute-done.upper_ref), channel_id=1, source_target_pairs={{0,32},{1,33},{2,34},{3,35},{4,36},{5,37},{6,38},{7,39},{8,40},{9,... | collective-permute-start | bytes 1548296 | tf_op jit(solution)/shard_map/ppermute | solution.py:39
  33.4 7.9 %collective-permute-start.7 = (bf16[480,1152]{1,0:T(8,128)(2,1)S(1)}, bf16[480,1152]{1,0:T(8,128)(2,1)S(1)}, u32[]{:S(2)}, u32[]{:S(2)}) collective-permute-start(bf16[480,1152]{1,0:T(8,128)(2,1)S(1)} %constant_dynamic-update-slice_fusion.2.refs_1_), channel_id=1, source_target_pairs={{0,1},{1,0},{2,3},{3,2},{4,5},{5,4},{6,7},{7,6},{8,9},{9,8},{10,11... | collective-permute-start | bytes 3317768 | tf_op jit(solution)/shard_map/ppermute | solution.py:39
  36.4 28.2 %copy-start.18 = (s32[16]{0:T(128)S(1)}, s32[16]{0:T(128)}, u32[]{:S(2)}) copy-start(s32[16]{0:T(128)} %constant.24.clone) | copy-start | bytes 196
  36.4 28.2 %copy-start.19 = (s32[16]{0:T(128)S(1)}, s32[16]{0:T(128)}, u32[]{:S(2)}) copy-start(s32[16]{0:T(128)} %constant.25.clone) | copy-start | bytes 196
  36.4 3.9 %collective-permute-start.6 = (bf16[448,1152]{1,0:T(8,128)(2,1)S(1)}, bf16[448,1152]{1,0:T(8,128)(2,1)S(1)}, u32[]{:S(2)}, u32[]{:S(2)}) collective-permute-start(bf16[448,1152]{1,0:T(8,128)(2,1)S(1)} %constant_dynamic-update-slice_fusion.refs_0_), channel_id=1, source_target_pairs={{0,1},{1,0},{2,3},{3,2},{4,5},{5,4},{6,7},{7,6},{8,9},{9,8},{10,11... | collective-permute-start | bytes 3096584 | tf_op jit(solution)/shard_map/ppermute | solution.py:39
  36.5 26.5 %collective-permute-start.5 = (bf16[480,1152]{1,0:T(8,128)(2,1)S(1)}, bf16[480,1152]{1,0:T(8,128)(2,1)}, u32[]{:S(2)}, u32[]{:S(2)}) collective-permute-start(bf16[480,1152]{1,0:T(8,128)(2,1)S(1)} %constant_dynamic-update-slice_fusion.2.refs_1_), channel_id=1, source_target_pairs={{0,32},{1,33},{2,34},{3,35},{4,36},{5,37},{6,38},{7,39},{8,40},{9,... | collective-permute-start | bytes 3317768 | tf_op jit(solution)/shard_map/ppermute | solution.py:39
  38.1 25.0 %collective-permute-start.2 = (bf16[448,1152]{1,0:T(8,128)(2,1)S(1)}, bf16[448,1152]{1,0:T(8,128)(2,1)}, u32[]{:S(2)}, u32[]{:S(2)}) collective-permute-start(bf16[448,1152]{1,0:T(8,128)(2,1)S(1)} %constant_dynamic-update-slice_fusion.refs_0_), channel_id=1, source_target_pairs={{0,96},{1,97},{2,98},{3,99},{4,100},{5,101},{6,102},{7,103},{8,104... | collective-permute-start | bytes 3096584 | tf_op jit(solution)/shard_map/ppermute | solution.py:39
  63.0 5.6 %collective-permute-start.9 = (bf16[480,1152]{1,0:T(8,128)(2,1)}, bf16[480,1152]{1,0:T(8,128)(2,1)S(1)}, u32[]{:S(2)}, u32[]{:S(2)}) collective-permute-start(bf16[480,1152]{1,0:T(8,128)(2,1)} %collective-permute-done.5.refs_5_), channel_id=1, source_target_pairs={{0,1},{1,0},{2,3},{3,2},{4,5},{5,4},{6,7},{7,6},{8,9},{9,8},{10,11... | collective-permute-start | bytes 3317768 | tf_op jit(solution)/shard_map/ppermute | solution.py:39
  64.6 4.1 %collective-permute-start.8 = (bf16[448,1152]{1,0:T(8,128)(2,1)}, bf16[448,1152]{1,0:T(8,128)(2,1)S(1)}, u32[]{:S(2)}, u32[]{:S(2)}) collective-permute-start(bf16[448,1152]{1,0:T(8,128)(2,1)} %collective-permute-done.2.refs_4_), channel_id=1, source_target_pairs={{0,1},{1,0},{2,3},{3,2},{4,5},{5,4},{6,7},{7,6},{8,9},{9,8},{10,11... | collective-permute-start | bytes 3096584 | tf_op jit(solution)/shard_map/ppermute | solution.py:39
  136.2 101.5 %all-gather.12.cloned.1.call-start = ((), (), s32[]{:S(2)}) async-start(), calls=%async_computation.2 | async-start | bytes 3899392 | tf_op jit(solution)/shard_map/all_gather | solution.py:264
  147.7 36.8 %copy-start.10 = (bf16[896,512]{1,0:T(8,128)(2,1)}, bf16[896,512]{1,0:T(8,128)(2,1)S(1)}, u32[]{:S(2)}) copy-start(bf16[896,512]{1,0:T(8,128)(2,1)S(1)} %all-gather) | copy-start | bytes 2752516
  147.7 7.4 %collective-permute-start.10 = (bf16[4,224,512]{2,1,0:T(8,128)(2,1)S(1)}, bf16[4,224,512]{2,1,0:T(8,128)(2,1)S(1)}, u32[]{:S(2)}, u32[]{:S(2)}) collective-permute-start(bf16[4,224,512]{2,1,0:T(8,128)(2,1)S(1)} %bitcast.16), channel_id=1, source_target_pairs={{0,1},{1,0},{2,3},{3,2},{4,5},{5,4},{6,7},{7,6},{8,9},{9,8},{10,11... | collective-permute-start | bytes 2752520 | tf_op jit(solution)/shard_map/ppermute | solution.py:39
  155.1 29.4 %copy-start.15 = (bf16[4,224,512]{2,1,0:T(8,128)(2,1)}, bf16[4,224,512]{2,1,0:T(8,128)(2,1)S(1)}, u32[]{:S(2)}) copy-start(bf16[4,224,512]{2,1,0:T(8,128)(2,1)S(1)} %collective-permute-done.10.other_ref) | copy-start | bytes 2752516
  188.9 102.2 %all-gather.14.cloned.1.call-start = ((), (), s32[]{:S(2)}) async-start(), calls=%async_computation.3 | async-start | bytes 3899392 | tf_op jit(solution)/shard_map/all_gather | solution.py:264
  202.3 4.3 %collective-permute-start.11 = (bf16[4,224,448]{2,1,0:T(8,128)(2,1)S(1)}, bf16[4,224,448]{2,1,0:T(8,128)(2,1)S(1)}, u32[]{:S(2)}, u32[]{:S(2)}) collective-permute-start(bf16[4,224,448]{2,1,0:T(8,128)(2,1)S(1)} %bitcast.12), channel_id=1, source_target_pairs={{0,1},{1,0},{2,3},{3,2},{4,5},{5,4},{6,7},{7,6},{8,9},{9,8},{10,11... | collective-permute-start | bytes 2408456 | tf_op jit(solution)/shard_map/ppermute | solution.py:39
  225.7 3.8 collective-permute-start.12
  242.1 102.2 %all-gather.16.cloned.1.call-start = ((), (), s32[]{:S(2)}) async-start(), calls=%async_computation.4 | async-start | bytes 3899392 | tf_op jit(solution)/shard_map/all_gather | solution.py:264
  255.6 4.3 %collective-permute-start.13 = (bf16[4,224,448]{2,1,0:T(8,128)(2,1)S(1)}, bf16[4,224,448]{2,1,0:T(8,128)(2,1)S(1)}, u32[]{:S(2)}, u32[]{:S(2)}) collective-permute-start(bf16[4,224,448]{2,1,0:T(8,128)(2,1)S(1)} %bitcast.14), channel_id=1, source_target_pairs={{0,1},{1,0},{2,3},{3,2},{4,5},{5,4},{6,7},{7,6},{8,9},{9,8},{10,11... | collective-permute-start | bytes 2408456 | tf_op jit(solution)/shard_map/ppermute | solution.py:39
  278.9 3.8 collective-permute-start.14
  355.7 17.6 %collective-permute-start.15 = (bf16[448,1152]{1,0:T(8,128)(2,1)}, bf16[448,1152]{1,0:T(8,128)(2,1)S(1)}, u32[]{:S(2)}, u32[]{:S(2)}) collective-permute-start(bf16[448,1152]{1,0:T(8,128)(2,1)} %get-tuple-element.26), channel_id=1, source_target_pairs={{0,0},{1,16},{2,2},{3,18},{4,4},{5,20},{6,6},{7,22},{8,8},{9,24},{... | collective-permute-start | bytes 3096584 | tf_op jit(solution)/shard_map/ppermute | solution.py:39
  (17 other events, 118.4 us)
Sparse Core Ops, SparseCore 0:
  136.4 48.0 all-gather.9
  189.0 48.7 all-gather.11
  242.3 48.7 all-gather.13
  295.6 48.7 all-gather.15
